TPU v7x, 32 devices: a whole 2x2x4 slice. The times are simulated.
32 devices in a mesh: ep: 16 (over z, y, x), os: 2 (over core).
Axes of the slice: x: 2, y: 2, z: 4, core: 2. Of those that a mesh axis runs over, the one named last changes fastest.
Arguments:
- tokens: bfloat16 [2048, 2048], P('ep', 'os'), may hold values from -6 to 6
- cotangent: bfloat16 [2048, 2048], P('ep', 'os'), may hold values from -6 to 6
- expert_ids: int32 [2048, 8], P('ep'), may hold values from 0 to 15, all different within a row; in each aligned block of 128 rows (0 to 127, 128 to 255, ...) at most 96 rows name the same one
- route_weight: float32 [2048, 8], P('ep'), may hold values from 0.1 to 1
- placement: int32 [16], replicated, may hold values from 0 to 15, each once
- swap_flags: int32 [2, 16], replicated, may hold values from 0 to 1, as said below
- params: bfloat16 [16, 3, 2048, 384], P('ep', None, 'os'), may hold values from -1 to 1
- first_moment: bfloat16 [16, 3, 2048, 384], P('ep', None, 'os'), may hold values from -6 to 6
- second_moment: bfloat16 [16, 3, 2048, 384], P('ep', None, 'os'), may hold values from 0.5 to 20
Outputs:
- mixed: bfloat16 [2048, 2048], P('ep', 'os')
- input_grad: bfloat16 [2048, 2048], P('ep', 'os')
- new_params: bfloat16 [16, 3, 2048, 384], P('ep', None, 'os')
- new_first: bfloat16 [16, 3, 2048, 384], P('ep', None, 'os')
- new_second: bfloat16 [16, 3, 2048, 384], P('ep', None, 'os')
Inputs may be any that keep to these rules, and one draw needn't show every extreme that they name: `expert_ids`: each row names 8 different experts; in each aligned block of 128 rows (the rows of one index of ep) no expert is named by more than 96 rows, a bound that some block reaches. `placement`: A permutation of the 16 expert ids. swap_flags[r, i] = swap_flags[r, i XOR 2^b_r] with b_0 = log2(16) - 1 and b_1 = 0.
All inputs are finite; a program needn't handle non-finite values.
Results may differ from a plain program's by a relative error of at most 0.023.
Values may be sent and summed in bfloat16 or wider, within the bound.
No kernel may reach another device: no remote copies, remote signals or barrier semaphores. Data moves between devices by JAX's collectives and lax.ppermute only.
A program may use at most 128 MiB of HBM per device.

v0:
```python
import jax
import jax.numpy as jnp
from jax import lax
from jax.sharding import PartitionSpec as P

beta_first = 0.9
beta_second = 0.999
learn_rate = 0.01
adam_eps = 1e-08
adam_count = 10.0


def from_partner(value, axis, bit):
    return lax.ppermute(value, axis, [(i, i ^ 1 << bit) for i in range(lax.axis_size(axis))])


def adam_update(weight, first, second, grad):
    first_new = beta_first * first.astype(jnp.float32) + (1.0 - beta_first) * grad
    second_new = beta_second * second.astype(jnp.float32) + (1.0 - beta_second) * grad * grad
    first_hat = first_new / (1.0 - beta_first**adam_count)
    second_hat = second_new / (1.0 - beta_second**adam_count)
    weight_new = weight.astype(jnp.float32) - learn_rate * first_hat / (
        jnp.sqrt(second_hat) + adam_eps
    )
    return (
        weight_new.astype(jnp.bfloat16),
        first_new.astype(jnp.bfloat16),
        second_new.astype(jnp.bfloat16),
    )


def derivative(back, gate, up):
    sigma = jax.nn.sigmoid(gate)
    active = gate * sigma
    d_gate = (back * up * sigma * (1.0 + gate * (1.0 - sigma))).astype(jnp.bfloat16)
    d_up = (back * active).astype(jnp.bfloat16)
    return jnp.stack((d_gate, d_up), axis=1)


def activate(gate, up):
    sigma = jax.nn.sigmoid(gate)
    return (gate * sigma * up).astype(jnp.bfloat16)


def on_device(
    tokens,
    cotangent,
    expert_ids,
    route_weight,
    placement,
    swap_flags,
    params,
    first_moment,
    second_moment,
):
    experts = lax.axis_size("ep")
    mine = lax.axis_index("ep")
    tok_rows, shard = tokens.shape
    top = expert_ids.shape[1]
    capacity = max(2, 3 * tok_rows * top // (2 * experts))
    index = jnp.arange(experts, dtype=jnp.int32)
    bits = [experts.bit_length() - 2, 0]
    place = placement
    own_flags = []
    for rnd in range(len(bits)):
        partner = index ^ 1 << bits[rnd]
        chosen = swap_flags[rnd] == 1
        place = jnp.where(chosen, place[partner], place)
        own_flags.append(jnp.sum(jnp.where(index == mine, swap_flags[rnd], 0)) == 1)
    held = params
    for rnd in range(len(bits)):
        moved = from_partner(held, "ep", bits[rnd])
        held = jnp.where(own_flags[rnd], moved, held)
    weight = held[0]
    flat_ids = expert_ids.reshape(-1)
    match = flat_ids[:, None] == place[None, :]
    dest = jnp.sum(jnp.where(match, index[None, :], 0), axis=1)
    counts = jnp.cumsum(match.astype(jnp.int32), axis=0)
    slot = jnp.sum(jnp.where(match, counts - 1, 0), axis=1)
    position = dest * capacity + slot
    num_rows = flat_ids.shape[0]
    table = (
        jnp.zeros((experts * capacity,), jnp.int32)
        .at[position]
        .set(jnp.arange(num_rows, dtype=jnp.int32) + 1)
    )
    filled = table > 0
    source = jnp.maximum(table - 1, 0)
    owner = source // top
    weights_flat = route_weight.reshape(-1)
    x_send = jnp.where(filled[:, None], tokens[owner], jnp.zeros((), jnp.bfloat16)).reshape(
        experts, capacity, shard
    )
    dy_send = jnp.where(
        filled[:, None], weights_flat[source][:, None] * cotangent[owner].astype(jnp.float32), 0.0
    )
    dy_send = dy_send.astype(jnp.bfloat16).reshape(experts, capacity, shard)
    x_recv = lax.all_to_all(x_send, "ep", split_axis=0, concat_axis=0, tiled=True)
    x_rows = x_recv.reshape(-1, shard)
    terms = jnp.einsum("rd,kdh->rkh", x_rows, weight[:2], preferred_element_type=jnp.float32)
    summed = lax.psum(terms.astype(jnp.bfloat16), "os").astype(jnp.float32)
    gate = summed[:, 0]
    up = summed[:, 1]
    hidden = activate(gate, up)
    rows_out = jnp.einsum(
        "rh,dh->rd", hidden, weight[2], preferred_element_type=jnp.float32
    ).astype(jnp.bfloat16)
    back_y = lax.all_to_all(
        rows_out.reshape(experts, capacity, shard), "ep", split_axis=0, concat_axis=0, tiled=True
    )
    dy_recv = lax.all_to_all(dy_send, "ep", split_axis=0, concat_axis=0, tiled=True)
    dy_rows = dy_recv.reshape(-1, shard)
    back_terms = jnp.einsum("rd,dh->rh", dy_rows, weight[2], preferred_element_type=jnp.float32)
    back = lax.psum(back_terms.astype(jnp.bfloat16), "os").astype(jnp.float32)
    deriv = derivative(back, gate, up)
    grad_in = jnp.einsum("rd,rkh->kdh", x_rows, deriv, preferred_element_type=jnp.float32)
    grad_out = jnp.einsum("rd,rh->dh", dy_rows, hidden, preferred_element_type=jnp.float32)
    grad = jnp.concatenate((grad_in, grad_out[None]), axis=0)
    rows_grad = jnp.einsum(
        "rkh,kdh->rd", deriv, weight[:2], preferred_element_type=jnp.float32
    ).astype(jnp.bfloat16)
    back_dx = lax.all_to_all(
        rows_grad.reshape(experts, capacity, shard), "ep", split_axis=0, concat_axis=0, tiled=True
    )
    picked_y = back_y.reshape(-1, shard)[position].reshape(tok_rows, top, shard)
    mixed = jnp.sum(route_weight[:, :, None] * picked_y.astype(jnp.float32), axis=1).astype(
        jnp.bfloat16
    )
    picked_dx = back_dx.reshape(-1, shard)[position].reshape(tok_rows, top, shard)
    input_grad = jnp.sum(picked_dx.astype(jnp.float32), axis=1).astype(jnp.bfloat16)
    moments = jnp.stack((first_moment, second_moment))
    for rnd in range(len(bits)):
        moved = from_partner(moments, "ep", bits[rnd])
        moments = jnp.where(own_flags[rnd], moved, moments)
    first = moments[0, 0]
    second = moments[1, 0]
    new_params, new_first, new_second = adam_update(weight, first, second, grad)
    return (mixed, input_grad, new_params[None], new_first[None], new_second[None])


def solution(mesh):
    placed = (
        P("ep", "os"),
        P("ep", "os"),
        P("ep", None),
        P("ep", None),
        P(),
        P(),
        P("ep", None, "os", None),
        P("ep", None, "os", None),
        P("ep", None, "os", None),
    )
    return jax.shard_map(
        on_device,
        mesh=mesh,
        in_specs=placed,
        out_specs=(
            P("ep", "os"),
            P("ep", "os"),
            P("ep", None, "os", None),
            P("ep", None, "os", None),
            P("ep", None, "os", None),
        ),
        check_vma=False,
    )
```

profile of v0, /device:TPU:0, one launch (start us, length us, event | category | flops | bytes accessed | tf_op | source)
XLA Modules:
  0.0 748.3 jit_solution(1478734096855744670)
XLA Ops:
  7.2 0.0 copy-start
  7.2 0.8 copy.20
  8.0 0.1 eq.51
  8.1 0.1 eq.45
  8.3 1.3 gather_fusion
  9.6 1.4 fusion.23
  11.0 0.7 gather_fusion.1
  11.6 0.7 compare_select_fusion.7
  12.3 0.1 compare_convert_fusion
  12.4 4.5 reduce-window.6
  16.9 0.1 slice.63
  17.0 0.1 copy.22
  17.2 0.1 copy.23
  17.3 0.1 add_add_fusion
  17.4 0.1 fusion.18
  17.5 4.3 scatter_custom_fusion
  21.8 0.8 copy.19
  22.6 0.1 reshape.332
  22.7 0.1 broadcast_in_dim.65
  22.8 5.8 gather_fusion.4
  28.7 0.1 mul.168
  28.7 5.1 gather_fusion.5
  33.8 2.1 fusion.1
  36.0 8.5 %all-to-all-start.2 = ((bf16[16,96,1024]{2,1,0:T(8,128)(2,1)}), bf16[16,96,1024]{2,1,0:T(8,128)(2,1)}, u32[]{:S(2)}, u32[]{:S(2)}) async-start(bf16[16,96,1024]{2,1,0:T(8,128)(2,1)} %fusion.1), calls=%async_computation.2 | async-start | bytes 6291456 | tf_op jit(solution)/shard_map/all_to_all | solution.py:111
  44.5 2.8 collective-permute-start
  47.2 5.1 gather_fusion.2
  52.3 1.8 broadcast_select_fusion.2
  54.1 101.8 %all-to-all-done.2 = bf16[16,96,1024]{2,1,0:T(8,128)(2,1)} async-done(((bf16[16,96,1024]{2,1,0:T(8,128)(2,1)}), bf16[16,96,1024]{2,1,0:T(8,128)(2,1)}, u32[]{:S(2)}, u32[]{:S(2)}) %all-to-all-start.2) | async-done | bytes 3145760 | tf_op jit(solution)/shard_map/all_to_all | solution.py:111
  156.0 16.5 %all-to-all-start = ((bf16[16,96,1024]{2,1,0:T(8,128)(2,1)}), bf16[16,96,1024]{2,1,0:T(8,128)(2,1)}, u32[]{:S(2)}, u32[]{:S(2)}) async-start(bf16[16,96,1024]{2,1,0:T(8,128)(2,1)} %broadcast_select_fusion.2), calls=%async_computation | async-start | bytes 6291456 | tf_op jit(solution)/shard_map/all_to_all | solution.py:98
  172.5 0.2 all-reduce.3.cloned.1.call-start
  173.4 77.9 %collective-permute-done = bf16[1,3,1024,384]{3,2,1,0:T(8,128)(2,1)} collective-permute-done((bf16[1,3,1024,384]{3,2,1,0:T(8,128)(2,1)}, bf16[1,3,1024,384]{3,2,1,0:T(8,128)(2,1)}, u32[]{:S(2)}, u32[]{:S(2)}) %collective-permute-start) | collective-permute-done | bytes 2359328 | tf_op jit(solution)/shard_map/ppermute | solution.py:14
  251.3 1.9 broadcast_select_fusion.3
  253.2 0.0 copy-start.10
  253.2 1.7 collective-permute-start.1
  255.5 57.4 %collective-permute-done.1 = bf16[1,3,1024,384]{3,2,1,0:T(8,128)(2,1)} collective-permute-done((bf16[1,3,1024,384]{3,2,1,0:T(8,128)(2,1)S(1)}, bf16[1,3,1024,384]{3,2,1,0:T(8,128)(2,1)}, u32[]{:S(2)}, u32[]{:S(2)}) %collective-permute-start.1) | collective-permute-done | bytes 2359328 | tf_op jit(solution)/shard_map/ppermute | solution.py:14
  313.0 1.9 broadcast_select_fusion.4
  314.9 5.6 convolution_convert_fusion.2
  320.5 5.9 convolution_convert_fusion.1
  326.4 0.0 all-reduce.3.cloned.1.call-update
  326.4 1.6 copy-done.4
  328.1 4.5 pad_maximum_fusion
  332.6 17.7 %all-reduce.3.cloned.1.call-done = (bf16[1536,2,384]{2,0,1:T(8,128)(2,1)}, bf16[1536,384]{1,0:T(8,128)(2,1)}) async-done(((bf16[1536,2,384]{2,0,1:T(8,128)(2,1)}, bf16[1536,384]{1,0:T(8,128)(2,1)}), (bf16[1536,2,384]{2,0,1:T(8,128)(2,1)}, bf16[1536,384]{1,0:T(8,128)(2,1)})) %all-reduce.3.cloned.1.call-update) | async-done | bytes 3538960 | tf_op jit(solution)/shard_map/psum | solution.py:101
  350.2 2.1 convert_element_type.118
  352.3 1.4 fusion.17
  353.8 1.0 copy-done.3
  354.7 1.0 copy-done.8
  355.8 4.1 bitcast_convert_fusion
  359.8 6.8 all-to-all-start.3
  366.6 200.8 %collective-permute-done.2 = bf16[2,1,3,1024,384]{4,3,2,1,0:T(8,128)(2,1)} collective-permute-done((bf16[2,1,3,1024,384]{4,3,2,1,0:T(8,128)(2,1)}, bf16[2,1,3,1024,384]{4,3,2,1,0:T(8,128)(2,1)}, u32[]{:S(2)}, u32[]{:S(2)}) %collective-permute-start.2) | collective-permute-done | bytes 4718624 | tf_op jit(solution)/shard_map/ppermute | solution.py:14
  567.4 6.6 broadcast_select_fusion
  574.0 3.0 multiply_convert_fusion
  577.1 1.0 copy-done.16
  578.1 4.6 convolution_convert_fusion
  582.7 8.2 %all-to-all-done.3 = bf16[16,96,1024]{2,1,0:T(8,128)(2,1)S(1)} async-done(((bf16[16,96,1024]{2,1,0:T(8,128)(2,1)}), bf16[16,96,1024]{2,1,0:T(8,128)(2,1)S(1)}, u32[]{:S(2)}, u32[]{:S(2)}) %all-to-all-start.3) | async-done | bytes 3145760 | tf_op jit(solution)/shard_map/all_to_all | solution.py:122
  590.8 16.1 %all-to-all-start.1 = ((bf16[16,96,1024]{2,1,0:T(8,128)(2,1)}), bf16[16,96,1024]{2,1,0:T(8,128)(2,1)}, u32[]{:S(2)}, u32[]{:S(2)}) async-start(bf16[16,96,1024]{2,1,0:T(8,128)(2,1)} %bitcast.119), calls=%async_computation.1 | async-start | bytes 6291456 | tf_op jit(solution)/shard_map/all_to_all | solution.py:108
  607.0 4.2 convolution_bitcast_fusion.1
  611.2 4.9 convolution_bitcast_fusion
  616.1 96.6 %collective-permute-done.3 = bf16[2,1,3,1024,384]{4,3,2,1,0:T(8,128)(2,1)} collective-permute-done((bf16[2,1,3,1024,384]{4,3,2,1,0:T(8,128)(2,1)}, bf16[2,1,3,1024,384]{4,3,2,1,0:T(8,128)(2,1)}, u32[]{:S(2)}, u32[]{:S(2)}) %collective-permute-start.3) | collective-permute-done | bytes 4718624 | tf_op jit(solution)/shard_map/ppermute | solution.py:14
  712.7 4.2 broadcast_select_fusion.1
  717.0 6.1 fusion.13
  723.0 5.3 gather_fusion.6
  728.4 3.7 bitcast_reduce_fusion
  732.1 7.3 gather_fusion.3
  739.4 2.0 fusion.3
  (45 shorter events, 0.2 us)
Async XLA Ops:
  7.2 21.6 %copy-start = (bf16[128,1024]{1,0:T(8,128)(2,1)S(1)}, bf16[128,1024]{1,0:T(8,128)(2,1)}, u32[]{:S(2)}) copy-start(bf16[128,1024]{1,0:T(8,128)(2,1)} %param.10) | copy-start | bytes 786436
  36.0 11.3 %copy-start.2 = (bf16[128,1024]{1,0:T(8,128)(2,1)S(1)}, bf16[128,1024]{1,0:T(8,128)(2,1)}, u32[]{:S(2)}) copy-start(bf16[128,1024]{1,0:T(8,128)(2,1)} %param.9) | copy-start | bytes 786436
  36.0 120.0 %all-to-all-start.2 = ((bf16[16,96,1024]{2,1,0:T(8,128)(2,1)}), bf16[16,96,1024]{2,1,0:T(8,128)(2,1)}, u32[]{:S(2)}, u32[]{:S(2)}) async-start(bf16[16,96,1024]{2,1,0:T(8,128)(2,1)} %fusion.1), calls=%async_computation.2 | async-start | bytes 6291456 | tf_op jit(solution)/shard_map/all_to_all | solution.py:111
  44.5 206.8 %collective-permute-start = (bf16[1,3,1024,384]{3,2,1,0:T(8,128)(2,1)}, bf16[1,3,1024,384]{3,2,1,0:T(8,128)(2,1)}, u32[]{:S(2)}, u32[]{:S(2)}) collective-permute-start(bf16[1,3,1024,384]{3,2,1,0:T(8,128)(2,1)} %param.15), channel_id=1, source_target_pairs={{0,16},{2,18},{4,20},{6,22},{8,24},{10,26},{12,28},{14,30},{16,0},... | collective-permute-start | bytes 7077896 | tf_op jit(solution)/shard_map/ppermute | solution.py:14
  156.0 164.5 %all-to-all-start = ((bf16[16,96,1024]{2,1,0:T(8,128)(2,1)}), bf16[16,96,1024]{2,1,0:T(8,128)(2,1)}, u32[]{:S(2)}, u32[]{:S(2)}) async-start(bf16[16,96,1024]{2,1,0:T(8,128)(2,1)} %broadcast_select_fusion.2), calls=%async_computation | async-start | bytes 6291456 | tf_op jit(solution)/shard_map/all_to_all | solution.py:98
  172.5 177.8 %all-reduce.3.cloned.1.call-start = ((), (), s32[]{:S(2)}) async-start(), calls=%async_computation.4 | async-start | bytes 7077888 | tf_op jit(solution)/shard_map/psum | solution.py:101
  253.2 2.3 copy-start.10
  253.2 59.8 %collective-permute-start.1 = (bf16[1,3,1024,384]{3,2,1,0:T(8,128)(2,1)S(1)}, bf16[1,3,1024,384]{3,2,1,0:T(8,128)(2,1)}, u32[]{:S(2)}, u32[]{:S(2)}) collective-permute-start(bf16[1,3,1024,384]{3,2,1,0:T(8,128)(2,1)S(1)} %broadcast_select_fusion.3), channel_id=1, source_target_pairs={{0,2},{2,0},{4,6},{6,4},{8,10},{10,8},{12,14},{14,12},{16,18},{18,... | collective-permute-start | bytes 7077896 | tf_op jit(solution)/shard_map/ppermute | solution.py:14
  314.9 5.6 copy-start.7
  326.4 1.7 copy-start.4
  332.6 234.9 %collective-permute-start.2 = (bf16[2,1,3,1024,384]{4,3,2,1,0:T(8,128)(2,1)}, bf16[2,1,3,1024,384]{4,3,2,1,0:T(8,128)(2,1)}, u32[]{:S(2)}, u32[]{:S(2)}) collective-permute-start(bf16[2,1,3,1024,384]{4,3,2,1,0:T(8,128)(2,1)} %pad_maximum_fusion), channel_id=1, source_target_pairs={{0,16},{2,18},{4,20},{6,22},{8,24},{10,26},{12,28},{14,30},{16,0},... | collective-permute-start | bytes 14155784 | tf_op jit(solution)/shard_map/ppermute | solution.py:14
  350.2 2.1 copy-start.15
  352.3 2.4 copy-start.3
  352.3 3.4 copy-start.8
  354.7 5.1 copy-start.11
  354.7 5.1 copy-start.13
  359.8 231.0 %all-to-all-start.3 = ((bf16[16,96,1024]{2,1,0:T(8,128)(2,1)}), bf16[16,96,1024]{2,1,0:T(8,128)(2,1)S(1)}, u32[]{:S(2)}, u32[]{:S(2)}) async-start(bf16[16,96,1024]{2,1,0:T(8,128)(2,1)} %bitcast.120), calls=%async_computation.3 | async-start | bytes 6291456 | tf_op jit(solution)/shard_map/all_to_all | solution.py:122
  574.0 138.7 %collective-permute-start.3 = (bf16[2,1,3,1024,384]{4,3,2,1,0:T(8,128)(2,1)}, bf16[2,1,3,1024,384]{4,3,2,1,0:T(8,128)(2,1)}, u32[]{:S(2)}, u32[]{:S(2)}) collective-permute-start(bf16[2,1,3,1024,384]{4,3,2,1,0:T(8,128)(2,1)} %broadcast_select_fusion), channel_id=1, source_target_pairs={{0,2},{2,0},{4,6},{6,4},{8,10},{10,8},{12,14},{14,12},{16,18},{18,... | collective-permute-start | bytes 14155784 | tf_op jit(solution)/shard_map/ppermute | solution.py:14
  577.1 1.0 copy-start.16
  590.8 141.3 %all-to-all-start.1 = ((bf16[16,96,1024]{2,1,0:T(8,128)(2,1)}), bf16[16,96,1024]{2,1,0:T(8,128)(2,1)}, u32[]{:S(2)}, u32[]{:S(2)}) async-start(bf16[16,96,1024]{2,1,0:T(8,128)(2,1)} %bitcast.119), calls=%async_computation.1 | async-start | bytes 6291456 | tf_op jit(solution)/shard_map/all_to_all | solution.py:108
  607.0 4.2 copy-start.12
  607.0 4.2 copy-start.14
  611.2 101.5 %copy-start.5 = (bf16[1,3,1024,384]{3,2,1,0:T(8,128)(2,1)S(1)}, bf16[1,3,1024,384]{3,2,1,0:T(8,128)(2,1)}, u32[]{:S(2)}) copy-start(bf16[1,3,1024,384]{3,2,1,0:T(8,128)(2,1)} %param.17) | copy-start | bytes 7077892
  611.2 101.5 %copy-start.6 = (bf16[1,3,1024,384]{3,2,1,0:T(8,128)(2,1)S(1)}, bf16[1,3,1024,384]{3,2,1,0:T(8,128)(2,1)}, u32[]{:S(2)}) copy-start(bf16[1,3,1024,384]{3,2,1,0:T(8,128)(2,1)} %param.16) | copy-start | bytes 7077892
  616.1 100.8 %copy-start.9 = (bf16[1,3,1024,384]{3,2,1,0:T(8,128)(2,1)S(1)}, bf16[1,3,1024,384]{3,2,1,0:T(8,128)(2,1)}, u32[]{:S(2)}) copy-start(bf16[1,3,1024,384]{3,2,1,0:T(8,128)(2,1)} %copy-done.7) | copy-start | bytes 7077892
  732.1 9.3 %copy-start.1 = (bf16[128,1024]{1,0:T(8,128)(2,1)S(1)}, bf16[128,1024]{1,0:T(8,128)(2,1)}, u32[]{:S(2)}) copy-start(bf16[128,1024]{1,0:T(8,128)(2,1)} %param.10) | copy-start | bytes 786436
Sparse Core Ops, SparseCore 0:
  326.6 23.6 all-reduce.2
where the time goes:
time: 749 us; the launch traced here: 748 us
  waiting for transfers between devices  560 us (75%)
  starting transfers between devices  52.6 us (7%)
  other arithmetic  48.4 us (6%)
  local copies, waits for them, and re-layouts  41.9 us (6%)
  matrix products  29.2 us (4%)
  between operations  15.7 us (2%)
    ppermute x4, waiting for transfers between devices, from_partner(): lax.ppermute(value, axis, [(i, i ^ 1 << bit) for i in range(lax.axis_size...  433 us
    all_to_all x1, waiting for transfers between devices, on_device(): lax.all_to_all(dy_send, 'ep', split_axis=0, concat_axis=0, tiled=True)  102 us
    psum x1, waiting for transfers between devices, on_device(): summed = lax.psum(terms.astype(jnp.bfloat16), 'os').astype(jnp.float32)  17.7 us
    all_to_all x1, starting transfers between devices, on_device(): lax.all_to_all(x_send, 'ep', split_axis=0, concat_axis=0, tiled=True)  16.5 us
    all_to_all x1, starting transfers between devices, on_device(): lax.all_to_all(rows_out.reshape(experts, capacity, shard), 'ep', split_ax...  16.1 us
  transfers between devices with their start and end apart: 9, of which 7 were waited for; matrix products, arithmetic and copies ran while one was open for 9% of the time, Pallas kernels for 0%

commit v1 on v0

v1 whole, which is shorter than its diff:
```python
import jax
import jax.numpy as jnp
from jax import lax
from jax.sharding import PartitionSpec as P

beta_first = 0.9
beta_second = 0.999
learn_rate = 0.01
adam_eps = 1e-08
adam_count = 10.0


def from_partner(value, bit):
    return lax.ppermute(value, "ep", [(i, i ^ bit) for i in range(lax.axis_size("ep"))])


def sum_over_cores(value):
    if lax.axis_size("os") != 2:
        return lax.psum(value, "os").astype(jnp.float32)
    moved = lax.ppermute(value, "os", [(0, 1), (1, 0)])
    return value.astype(jnp.float32) + moved.astype(jnp.float32)


def adam_update(weight, first, second, grad):
    first_new = beta_first * first.astype(jnp.float32) + (1.0 - beta_first) * grad
    second_new = beta_second * second.astype(jnp.float32) + (1.0 - beta_second) * grad * grad
    first_hat = first_new / (1.0 - beta_first**adam_count)
    second_hat = second_new / (1.0 - beta_second**adam_count)
    weight_new = weight.astype(jnp.float32) - learn_rate * first_hat / (
        jnp.sqrt(second_hat) + adam_eps
    )
    return (
        weight_new.astype(jnp.bfloat16),
        first_new.astype(jnp.bfloat16),
        second_new.astype(jnp.bfloat16),
    )


def high_bits(experts):
    return [1 << b for b in range(experts.bit_length() - 2, 1, -1)]


def block_order(experts):
    order = [0]
    for bit in high_bits(experts):
        order = order + [r ^ bit for r in order]
    return [r ^ low for low in range(4) for r in order]


def gather_rows(block):
    experts = lax.axis_size("ep")
    for bit in high_bits(experts):
        block = jnp.concatenate((block, from_partner(block, bit)), axis=0)
    half = block.shape[1] // 2
    one = from_partner(block, 1)
    two = from_partner(block, 2)
    three = jnp.concatenate(
        (from_partner(two[:, :half], 1), from_partner(one[:, half:], 2)), axis=1
    )
    return jnp.concatenate((block, one, two, three), axis=0)


def add_rounded(*parts):
    total = parts[0].astype(jnp.float32)
    for part in parts[1:]:
        total = total + part.astype(jnp.float32)
    return total.astype(jnp.bfloat16)


def scatter_rows(rows):
    experts = lax.axis_size("ep")
    size = rows.shape[0] // 4
    half = rows.shape[1] // 2
    own, one, two, three = (rows[k * size : (k + 1) * size] for k in range(4))
    two_left = add_rounded(two[:, :half], from_partner(three[:, :half], 1))
    one_right = add_rounded(one[:, half:], from_partner(three[:, half:], 2))
    left = add_rounded(own[:, :half], from_partner(one[:, :half], 1), from_partner(two_left, 2))
    right = add_rounded(own[:, half:], from_partner(one_right, 1), from_partner(two[:, half:], 2))
    block = jnp.concatenate((left, right), axis=1)
    for bit in reversed(high_bits(experts)):
        keep = block.shape[0] // 2
        block = add_rounded(block[:keep], from_partner(block[keep:], bit))
    return block


def migrate(parts, own_flags, bits):
    result = []
    for part in parts:
        for rnd, bit in enumerate(bits):
            moved = from_partner(part, bit)
            part = jnp.where(own_flags[rnd], moved, part)
        result.append(part)
    return result


def dot(a, b, dims):
    return lax.dot_general(a, b, ((dims[:1], dims[1:]), ((), ())), preferred_element_type=jnp.float32)


def on_device(
    tokens,
    cotangent,
    expert_ids,
    route_weight,
    placement,
    swap_flags,
    params,
    first_moment,
    second_moment,
):
    experts = lax.axis_size("ep")
    mine = lax.axis_index("ep")
    index = jnp.arange(experts, dtype=jnp.int32)
    bits = [experts // 2, 1]
    place = placement
    own_flags = []
    for rnd in range(len(bits)):
        place = jnp.where(swap_flags[rnd] == 1, place[index ^ bits[rnd]], place)
        own_flags.append(swap_flags[rnd, mine] == 1)
    dense = jnp.sum(
        jnp.where(
            expert_ids.T[None, :, :] == index[:, None, None], route_weight.T[None, :, :], 0.0
        ),
        axis=1,
    )
    dense = lax.all_gather(dense, "ep")
    scale = lax.dynamic_index_in_dim(dense, place[mine], axis=1, keepdims=False)
    scale = scale[mine ^ jnp.array(block_order(experts), jnp.int32)].reshape(-1, 1)

    weight = migrate([params[0, k] for k in range(3)], own_flags, bits)
    x_rows = gather_rows(tokens)
    dy_rows = (scale * gather_rows(cotangent).astype(jnp.float32)).astype(jnp.bfloat16)

    gate = sum_over_cores(dot(x_rows, weight[0], (1, 0)).astype(jnp.bfloat16))
    up = sum_over_cores(dot(x_rows, weight[1], (1, 0)).astype(jnp.bfloat16))
    sigma = jax.nn.sigmoid(gate)
    active = gate * sigma
    hidden = (active * up).astype(jnp.bfloat16)
    mixed = scatter_rows((scale * dot(hidden, weight[2], (1, 1))).astype(jnp.bfloat16))

    back = sum_over_cores(dot(dy_rows, weight[2], (1, 0)).astype(jnp.bfloat16))
    d_gate = (back * up * sigma * (1.0 + gate * (1.0 - sigma))).astype(jnp.bfloat16)
    d_up = (back * active).astype(jnp.bfloat16)
    rows_grad = dot(d_gate, weight[0], (1, 1)) + dot(d_up, weight[1], (1, 1))
    input_grad = scatter_rows(rows_grad.astype(jnp.bfloat16))
    grad = [
        dot(x_rows, d_gate, (0, 0)),
        dot(x_rows, d_up, (0, 0)),
        dot(dy_rows, hidden, (0, 0)),
    ]
    first = migrate([first_moment[0, k] for k in range(3)], own_flags, bits)
    second = migrate([second_moment[0, k] for k in range(3)], own_flags, bits)
    updated = [adam_update(*state) for state in zip(weight, first, second, grad)]
    new_params, new_first, new_second = (jnp.stack(part)[None] for part in zip(*updated))
    return (mixed, input_grad, new_params, new_first, new_second)


def solution(mesh):
    state = P("ep", None, "os", None)
    rows = P("ep", "os")
    return jax.shard_map(
        on_device,
        mesh=mesh,
        in_specs=(rows, rows, P("ep", None), P("ep", None), P(), P(), state, state, state),
        out_specs=(rows, rows, state, state, state),
        check_vma=False,
    )
```

time: 749 us -> 642 us (0.86)
  waiting for transfers between devices: 560 us -> 389 us
  blocking collectives: 0 us -> 131 us
  other arithmetic: 48.4 us -> 19.1 us
  local copies, waits for them, and re-layouts: 41.9 us -> 15 us
  between operations: 15.7 us -> 4.53 us
    all_gather x0 -> x1, blocking collectives: none -> 131 us  [on_device(): dense = lax.all_gather(dense, 'ep')]
    all_to_all x4 -> x0, waiting for transfers between devices: 110 us -> none  [the longest x1 102 us: on_device(): lax.all_to_all(dy_send, 'ep', split_axis=0, concat_axis=0, tiled=True)]
    ppermute x4 -> x49, starting transfers between devices: 4.45 us -> 56.7 us  [the longest x46 56.6 us: from_partner(): lax.ppermute(value, 'ep', [(i, i ^ bit) for i in range(lax.axis_size('ep'...]
    all_to_all x4 -> x0, starting transfers between devices: 47.9 us -> none  [the longest x1 16.5 us: on_device(): lax.all_to_all(x_send, 'ep', split_axis=0, concat_axis=0, tiled=True)]
    ppermute x4 -> x49, waiting for transfers between devices: 433 us -> 389 us  [the longest x46 388 us: from_partner(): lax.ppermute(value, 'ep', [(i, i ^ bit) for i in range(lax.axis_size('ep'...]
    gather x7 -> x3, local copies, waits for them, and re-layouts: 30.6 us -> 1.88 us  [the longest x2 1.32 us: on_device(): place = jnp.where(swap_flags[rnd] == 1, place[index ^ bits[rnd]], place)]
    psum x1 -> x0, waiting for transfers between devices: 17.7 us -> none  [on_device(): summed = lax.psum(terms.astype(jnp.bfloat16), 'os').astype(jnp.float32)]
    select_n x9, other arithmetic: 17.2 us -> 3.91 us  [the longest x5 3.89 us: migrate(): part = jnp.where(own_flags[rnd], moved, part)]
  transfers between devices with their start and end apart: 9 -> 49, of which waited for: 7 -> 27; matrix products, arithmetic and copies ran while one was open for 9% -> 7% of each run, Pallas kernels for 0% -> 0%
where the time goes in v1:
time: 642 us
  waiting for transfers between devices  389 us (61%)
  blocking collectives  131 us (20%)
  starting transfers between devices  56.7 us (9%)
  matrix products  25.6 us (4%)
  other arithmetic  19.1 us (3%)
  local copies, waits for them, and re-layouts  15 us (2%)
    ppermute x46, waiting for transfers between devices, from_partner(): lax.ppermute(value, 'ep', [(i, i ^ bit) for i in range(lax.axis_size('ep'...  388 us
    all_gather x1, blocking collectives, on_device(): dense = lax.all_gather(dense, 'ep')  131 us
    ppermute x46, starting transfers between devices, from_partner(): lax.ppermute(value, 'ep', [(i, i ^ bit) for i in range(lax.axis_size('ep'...  56.6 us
    dot_general x9, matrix products, dot(): lax.dot_general(a, b, ((dims[:1], dims[1:]), ((), ())), preferred_element...  25.6 us
  transfers between devices with their start and end apart: 49, of which 27 were waited for; matrix products, arithmetic and copies ran while one was open for 7% of the time, Pallas kernels for 0%

profile of v1, /device:TPU:0, one launch (start us, length us, event | category | flops | bytes accessed | tf_op | source)
XLA Modules:
  0.0 641.6 jit_solution(7283180837865897559)
XLA Ops:
  0.6 1.1 copy.30
  1.8 4.1 collective-permute-start.22
  5.9 3.1 slice_bitcast_fusion.7
  9.2 2.8 collective-permute-start.6
  12.1 2.8 collective-permute-start
  18.8 131.3 %all-gather = f32[256,128]{1,0:T(8,128)S(1)} all-gather(f32[16,128]{1,0:T(8,128)S(1)} %select_reduce_fusion), channel_id=2, replica_groups=mesh['ep'=16,'os'=2] {'ep'}, dimensions={0}, use_global_device_ids=true | all-gather | bytes 139264 | tf_op jit(solution)/shard_map/all_gather | solution.py:126
  152.3 5.0 collective-permute-start.23
  157.3 3.0 broadcast_select_fusion.7
  161.0 1.9 pad_maximum_fusion.3
  165.2 1.1 constant_dynamic-update-slice_fusion.1
  166.3 4.0 collective-permute-done.23
  170.4 1.1 pad_maximum_fusion
  171.5 1.7 collective-permute-start.24
  173.2 1.7 collective-permute-start.25
  176.0 1.1 constant_dynamic-update-slice_fusion
  177.1 1.7 collective-permute-start.2
  178.8 1.7 collective-permute-start.3
  183.3 52.4 %collective-permute-done.7 = bf16[1024,384]{1,0:T(8,128)(2,1)S(1)} collective-permute-done((bf16[1024,384]{1,0:T(8,128)(2,1)S(1)}, bf16[1024,384]{1,0:T(8,128)(2,1)S(1)}, u32[]{:S(2)}, u32[]{:S(2)}) %collective-permute-start.7) | collective-permute-done | bytes 786464 | tf_op jit(solution)/shard_map/ppermute | solution.py:14
  235.7 4.0 collective-permute-start.37
  239.9 3.0 collective-permute-start.45
  244.5 11.0 %collective-permute-done.26 = bf16[512,512]{0,1:T(8,128)(2,1)S(1)} collective-permute-done((bf16[512,512]{0,1:T(8,128)(2,1)S(1)}, bf16[512,512]{0,1:T(8,128)(2,1)S(1)}, u32[]{:S(2)}, u32[]{:S(2)}) %collective-permute-start.26) | collective-permute-done | bytes 524320 | tf_op jit(solution)/shard_map/ppermute | solution.py:14
  256.2 1.3 collective-permute-start.5
  257.7 2.4 fusion.3
  260.1 4.5 collective-permute-done.4
  265.6 2.4 convolution_convert_fusion.1
  268.3 32.1 %collective-permute-done.37 = bf16[1024,384]{1,0:T(8,128)(2,1)S(1)} collective-permute-done((bf16[1024,384]{1,0:T(8,128)(2,1)S(1)}, bf16[1024,384]{1,0:T(8,128)(2,1)S(1)}, u32[]{:S(2)}, u32[]{:S(2)}) %collective-permute-start.37) | collective-permute-done | bytes 786464 | tf_op jit(solution)/shard_map/ppermute | solution.py:14
  300.4 33.7 %collective-permute-done.41 = bf16[1024,384]{1,0:T(8,128)(2,1)S(1)} collective-permute-done((bf16[1024,384]{1,0:T(8,128)(2,1)S(1)}, bf16[1024,384]{1,0:T(8,128)(2,1)S(1)}, u32[]{:S(2)}, u32[]{:S(2)}) %collective-permute-start.41) | collective-permute-done | bytes 786464 | tf_op jit(solution)/shard_map/ppermute | solution.py:14
  334.1 33.7 %collective-permute-done.45 = bf16[1024,384]{1,0:T(8,128)(2,1)S(1)} collective-permute-done((bf16[1024,384]{1,0:T(8,128)(2,1)S(1)}, bf16[1024,384]{1,0:T(8,128)(2,1)S(1)}, u32[]{:S(2)}, u32[]{:S(2)}) %collective-permute-start.45) | collective-permute-done | bytes 786464 | tf_op jit(solution)/shard_map/ppermute | solution.py:14
  368.2 33.4 %collective-permute-done.39 = bf16[1024,384]{1,0:T(8,128)(2,1)S(1)} collective-permute-done((bf16[1024,384]{1,0:T(8,128)(2,1)S(1)}, bf16[1024,384]{1,0:T(8,128)(2,1)S(1)}, u32[]{:S(2)}, u32[]{:S(2)}) %collective-permute-start.39) | collective-permute-done | bytes 786464 | tf_op jit(solution)/shard_map/ppermute | solution.py:14
  402.3 16.1 %collective-permute-done.43 = bf16[1024,384]{1,0:T(8,128)(2,1)S(1)} collective-permute-done((bf16[1024,384]{1,0:T(8,128)(2,1)S(1)}, bf16[1024,384]{1,0:T(8,128)(2,1)S(1)}, u32[]{:S(2)}, u32[]{:S(2)}) %collective-permute-start.43) | collective-permute-done | bytes 786464 | tf_op jit(solution)/shard_map/ppermute | solution.py:14
  419.2 15.2 %collective-permute-done.47 = bf16[1024,384]{1,0:T(8,128)(2,1)S(1)} collective-permute-done((bf16[1024,384]{1,0:T(8,128)(2,1)S(1)}, bf16[1024,384]{1,0:T(8,128)(2,1)S(1)}, u32[]{:S(2)}, u32[]{:S(2)}) %collective-permute-start.47) | collective-permute-done | bytes 786464 | tf_op jit(solution)/shard_map/ppermute | solution.py:14
  435.4 1.3 multiply_convert_fusion.4
  436.7 16.7 %collective-permute-done.44 = bf16[1024,384]{1,0:T(8,128)(2,1)S(1)} collective-permute-done((bf16[1024,384]{1,0:T(8,128)(2,1)S(1)}, bf16[1024,384]{1,0:T(8,128)(2,1)S(1)}, u32[]{:S(2)}, u32[]{:S(2)}) %collective-permute-start.44) | collective-permute-done | bytes 786464 | tf_op jit(solution)/shard_map/ppermute | solution.py:14
  453.4 3.9 fusion.20
  457.3 2.4 convolution_convert_fusion
  459.8 2.4 fusion.28
  463.2 2.5 multiply_convert_fusion.5
  465.7 2.4 add_convert_fusion
  468.9 2.4 multiply_convert_fusion.1
  471.5 1.6 collective-permute-start.15
  473.6 1.5 collective-permute-start.48
  475.6 7.5 %collective-permute-done.30 = bf16[512,512]{0,1:T(8,128)(2,1)S(1)} collective-permute-done((bf16[512,512]{0,1:T(8,128)(2,1)S(1)}, bf16[512,512]{0,1:T(8,128)(2,1)S(1)}, u32[]{:S(2)}, u32[]{:S(2)}) %collective-permute-start.30) | collective-permute-done | bytes 524320 | tf_op jit(solution)/shard_map/ppermute | solution.py:14
  483.4 11.0 %collective-permute-done.15 = bf16[512,512]{0,1:T(8,128)(2,1)S(1)} collective-permute-done((bf16[512,512]{0,1:T(8,128)(2,1)S(1)}, bf16[512,512]{0,1:T(8,128)(2,1)S(1)}, u32[]{:S(2)}, u32[]{:S(2)}) %collective-permute-start.15) | collective-permute-done | bytes 524320 | tf_op jit(solution)/shard_map/ppermute | solution.py:14
  494.6 16.6 %collective-permute-done.46 = bf16[1024,384]{1,0:T(8,128)(2,1)S(1)} collective-permute-done((bf16[1024,384]{1,0:T(8,128)(2,1)S(1)}, bf16[1024,384]{1,0:T(8,128)(2,1)S(1)}, u32[]{:S(2)}, u32[]{:S(2)}) %collective-permute-start.46) | collective-permute-done | bytes 786464 | tf_op jit(solution)/shard_map/ppermute | solution.py:14
  511.7 16.3 %collective-permute-done.48 = bf16[1024,384]{1,0:T(8,128)(2,1)S(1)} collective-permute-done((bf16[1024,384]{1,0:T(8,128)(2,1)S(1)}, bf16[1024,384]{1,0:T(8,128)(2,1)S(1)}, u32[]{:S(2)}, u32[]{:S(2)}) %collective-permute-start.48) | collective-permute-done | bytes 786464 | tf_op jit(solution)/shard_map/ppermute | solution.py:14
  528.6 10.7 %collective-permute-done.29 = bf16[512,512]{0,1:T(8,128)(2,1)S(1)} collective-permute-done((bf16[512,512]{0,1:T(8,128)(2,1)S(1)}, bf16[512,512]{0,1:T(8,128)(2,1)S(1)}, u32[]{:S(2)}, u32[]{:S(2)}) %collective-permute-start.29) | collective-permute-done | bytes 524320 | tf_op jit(solution)/shard_map/ppermute | solution.py:14
  541.9 3.6 fusion.15
  545.8 37.6 %collective-permute-done.14 = bf16[512,512]{0,1:T(8,128)(2,1)S(1)} collective-permute-done((bf16[512,512]{0,1:T(8,128)(2,1)S(1)}, bf16[512,512]{0,1:T(8,128)(2,1)S(1)}, u32[]{:S(2)}, u32[]{:S(2)}) %collective-permute-start.14) | collective-permute-done | bytes 524320 | tf_op jit(solution)/shard_map/ppermute | solution.py:14
  583.5 2.0 collective-permute-start.19
  586.4 1.6 collective-permute-start.18
  588.0 3.8 fusion.13
  591.8 6.5 %collective-permute-done.34 = bf16[512,512]{0,1:T(8,128)(2,1)S(1)} collective-permute-done((bf16[512,512]{0,1:T(8,128)(2,1)S(1)}, bf16[512,512]{0,1:T(8,128)(2,1)S(1)}, u32[]{:S(2)}, u32[]{:S(2)}) %collective-permute-start.34) | collective-permute-done | bytes 524320 | tf_op jit(solution)/shard_map/ppermute | solution.py:14
  598.3 2.0 collective-permute-done.33
  600.6 1.4 collective-permute-start.35
  602.1 5.7 collective-permute-done.19
  607.8 1.5 collective-permute-done.18
  609.6 1.4 collective-permute-start.20
  611.0 1.7 maximum_bitcast_fusion.2
  612.7 1.7 maximum_bitcast_fusion.1
  614.6 3.5 collective-permute-start.36
  618.1 8.8 %collective-permute-done.20 = bf16[256,1024]{0,1:T(8,128)(2,1)S(1)} collective-permute-done((bf16[256,1024]{0,1:T(8,128)(2,1)S(1)}, bf16[256,1024]{0,1:T(8,128)(2,1)S(1)}, u32[]{:S(2)}, u32[]{:S(2)}) %collective-permute-start.20) | collective-permute-done | bytes 524320 | tf_op jit(solution)/shard_map/ppermute | solution.py:14
  627.1 2.3 collective-permute-start.21
  629.5 1.7 maximum_bitcast_fusion
  632.1 8.5 %collective-permute-done.21 = bf16[128,1024]{0,1:T(8,128)(2,1)S(1)} collective-permute-done((bf16[128,1024]{0,1:T(8,128)(2,1)S(1)}, bf16[128,1024]{0,1:T(8,128)(2,1)S(1)}, u32[]{:S(2)}, u32[]{:S(2)}) %collective-permute-start.21) | collective-permute-done | bytes 262176 | tf_op jit(solution)/shard_map/ppermute | solution.py:14
  (135 shorter events, 28.0 us)
Async XLA Ops:
  1.8 13.1 %copy-start = (s32[16]{0:T(128)S(1)}, s32[16]{0:T(128)}, u32[]{:S(2)}) copy-start(s32[16]{0:T(128)} %param.14) | copy-start | bytes 196
  1.8 13.8 %copy-start.9 = (s32[2,16]{1,0:T(2,128)S(1)}, s32[2,16]{1,0:T(2,128)}, u32[]{:S(2)}) copy-start(s32[2,16]{1,0:T(2,128)} %param.15) | copy-start | bytes 388
  1.8 17.0 %copy-start.10 = (f32[128,8]{0,1:T(8,128)S(1)}, f32[128,8]{0,1:T(8,128)}, u32[]{:S(2)}) copy-start(f32[128,8]{0,1:T(8,128)} %param.13) | copy-start | bytes 12292
  1.8 17.0 %copy-start.11 = (s32[128,8]{0,1:T(8,128)S(1)}, s32[128,8]{0,1:T(8,128)}, u32[]{:S(2)}) copy-start(s32[128,8]{0,1:T(8,128)} %param.12) | copy-start | bytes 12292
  1.8 149.6 %copy-start.12 = (s32[16]{0:T(128)S(1)}, s32[16]{0:T(128)}, u32[]{:S(2)}) copy-start(s32[16]{0:T(128)} %constant.54.clone) | copy-start | bytes 196
  1.8 155.5 %copy-start.1 = (bf16[1,3,1024,384]{3,2,1,0:T(8,128)(2,1)S(1)}, bf16[1,3,1024,384]{3,2,1,0:T(8,128)(2,1)}, u32[]{:S(2)}) copy-start(bf16[1,3,1024,384]{3,2,1,0:T(8,128)(2,1)} %param.16) | copy-start | bytes 7077892
  1.8 149.6 %collective-permute-start.22 = (bf16[128,1024]{0,1:T(8,128)(2,1)S(1)}, bf16[128,1024]{0,1:T(8,128)(2,1)S(1)}, u32[]{:S(2)}, u32[]{:S(2)}) collective-permute-start(bf16[128,1024]{0,1:T(8,128)(2,1)S(1)} %copy.30), channel_id=1, source_target_pairs={{0,16},{2,18},{4,20},{6,22},{8,24},{10,26},{12,28},{14,30},{16,0},... | collective-permute-start | bytes 786440 | tf_op jit(solution)/shard_map/ppermute | solution.py:14
  9.0 148.3 %collective-permute-start.12 = (bf16[1024,384]{1,0:T(8,128)(2,1)}, bf16[1024,384]{1,0:T(8,128)(2,1)}, u32[]{:S(2)}, u32[]{:S(2)}) collective-permute-start(bf16[1024,384]{1,0:T(8,128)(2,1)} %get-tuple-element.61), channel_id=1, source_target_pairs={{0,16},{2,18},{4,20},{6,22},{8,24},{10,26},{12,28},{14,30},{16,0},... | collective-permute-start | bytes 2359304 | tf_op jit(solution)/shard_map/ppermute | solution.py:14
  9.2 148.1 %collective-permute-start.6 = (bf16[1024,384]{1,0:T(8,128)(2,1)}, bf16[1024,384]{1,0:T(8,128)(2,1)}, u32[]{:S(2)}, u32[]{:S(2)}) collective-permute-start(bf16[1024,384]{1,0:T(8,128)(2,1)} %get-tuple-element.60), channel_id=1, source_target_pairs={{0,16},{2,18},{4,20},{6,22},{8,24},{10,26},{12,28},{14,30},{16,0},... | collective-permute-start | bytes 2359304 | tf_op jit(solution)/shard_map/ppermute | solution.py:14
  11.9 145.4 %collective-permute-start.9 = (bf16[1024,384]{1,0:T(8,128)(2,1)}, bf16[1024,384]{1,0:T(8,128)(2,1)}, u32[]{:S(2)}, u32[]{:S(2)}) collective-permute-start(bf16[1024,384]{1,0:T(8,128)(2,1)} %get-tuple-element.59), channel_id=1, source_target_pairs={{0,16},{2,18},{4,20},{6,22},{8,24},{10,26},{12,28},{14,30},{16,0},... | collective-permute-start | bytes 2359304 | tf_op jit(solution)/shard_map/ppermute | solution.py:14
  12.1 148.9 %collective-permute-start = (bf16[128,1024]{1,0:T(8,128)(2,1)}, bf16[128,1024]{1,0:T(8,128)(2,1)}, u32[]{:S(2)}, u32[]{:S(2)}) collective-permute-start(bf16[128,1024]{1,0:T(8,128)(2,1)} %param.10), channel_id=1, source_target_pairs={{0,16},{2,18},{4,20},{6,22},{8,24},{10,26},{12,28},{14,30},{16,0},... | collective-permute-start | bytes 786440 | tf_op jit(solution)/shard_map/ppermute | solution.py:14
  151.4 5.9 copy-start.4
  152.3 18.0 %collective-permute-start.23 = (bf16[256,1024]{0,1:T(8,128)(2,1)}, bf16[256,1024]{0,1:T(8,128)(2,1)}, u32[]{:S(2)}, u32[]{:S(2)}) collective-permute-start(bf16[256,1024]{0,1:T(8,128)(2,1)} %pad_maximum_fusion.4), channel_id=1, source_target_pairs={{0,8},{2,10},{4,12},{6,14},{8,0},{10,2},{12,4},{14,6},{16,24},{18,... | collective-permute-start | bytes 1572872 | tf_op jit(solution)/shard_map/ppermute | solution.py:14
  160.3 10.0 %copy-start.5 = (bf16[128,1024]{0,1:T(8,128)(2,1)S(1)}, bf16[128,1024]{0,1:T(8,128)(2,1)}, u32[]{:S(2)}) copy-start(bf16[128,1024]{0,1:T(8,128)(2,1)} %copy-done.4) | copy-start | bytes 786436
  160.3 20.7 %collective-permute-start.13 = (bf16[1024,384]{1,0:T(8,128)(2,1)}, bf16[1024,384]{1,0:T(8,128)(2,1)S(1)}, u32[]{:S(2)}, u32[]{:S(2)}) collective-permute-start(bf16[1024,384]{1,0:T(8,128)(2,1)} %get-tuple-element.57), channel_id=1, source_target_pairs={{0,2},{2,0},{4,6},{6,4},{8,10},{10,8},{12,14},{14,12},{16,18},{18,... | collective-permute-start | bytes 2359304 | tf_op jit(solution)/shard_map/ppermute | solution.py:14
  162.9 13.1 %collective-permute-start.1 = (bf16[256,1024]{1,0:T(8,128)(2,1)}, bf16[256,1024]{1,0:T(8,128)(2,1)}, u32[]{:S(2)}, u32[]{:S(2)}) collective-permute-start(bf16[256,1024]{1,0:T(8,128)(2,1)} %pad_maximum_fusion.3), channel_id=1, source_target_pairs={{0,8},{2,10},{4,12},{6,14},{8,0},{10,2},{12,4},{14,6},{16,24},{18,... | collective-permute-start | bytes 1572872 | tf_op jit(solution)/shard_map/ppermute | solution.py:14
  165.2 16.5 %copy-start.2 = (bf16[1,3,1024,384]{3,2,1,0:T(8,128)(2,1)S(1)}, bf16[1,3,1024,384]{3,2,1,0:T(8,128)(2,1)}, u32[]{:S(2)}) copy-start(bf16[1,3,1024,384]{3,2,1,0:T(8,128)(2,1)} %param.17) | copy-start | bytes 7077892
  171.5 68.4 %collective-permute-start.24 = (bf16[512,1024]{0,1:T(8,128)(2,1)S(1)}, bf16[512,1024]{0,1:T(8,128)(2,1)S(1)}, u32[]{:S(2)}, u32[]{:S(2)}) collective-permute-start(bf16[512,1024]{0,1:T(8,128)(2,1)S(1)} %pad_maximum_fusion), channel_id=1, source_target_pairs={{0,2},{2,0},{4,6},{6,4},{8,10},{10,8},{12,14},{14,12},{16,18},{18,... | collective-permute-start | bytes 3145736 | tf_op jit(solution)/shard_map/ppermute | solution.py:14
  173.2 66.6 %collective-permute-start.25 = (bf16[512,1024]{0,1:T(8,128)(2,1)S(1)}, bf16[512,1024]{0,1:T(8,128)(2,1)S(1)}, u32[]{:S(2)}, u32[]{:S(2)}) collective-permute-start(bf16[512,1024]{0,1:T(8,128)(2,1)S(1)} %pad_maximum_fusion), channel_id=1, source_target_pairs={{0,4},{2,6},{4,0},{6,2},{8,12},{10,14},{12,8},{14,10},{16,20},{18,... | collective-permute-start | bytes 3145736 | tf_op jit(solution)/shard_map/ppermute | solution.py:14
  177.1 66.8 %collective-permute-start.2 = (bf16[512,1024]{1,0:T(8,128)(2,1)S(1)}, bf16[512,1024]{1,0:T(8,128)(2,1)S(1)}, u32[]{:S(2)}, u32[]{:S(2)}) collective-permute-start(bf16[512,1024]{1,0:T(8,128)(2,1)S(1)} %get-tuple-element.62), channel_id=1, source_target_pairs={{0,2},{2,0},{4,6},{6,4},{8,10},{10,8},{12,14},{14,12},{16,18},{18,... | collective-permute-start | bytes 3145736 | tf_op jit(solution)/shard_map/ppermute | solution.py:14
  178.8 64.2 %collective-permute-start.3 = (bf16[512,1024]{1,0:T(8,128)(2,1)S(1)}, bf16[512,1024]{1,0:T(8,128)(2,1)S(1)}, u32[]{:S(2)}, u32[]{:S(2)}) collective-permute-start(bf16[512,1024]{1,0:T(8,128)(2,1)S(1)} %get-tuple-element.62), channel_id=1, source_target_pairs={{0,4},{2,6},{4,0},{6,2},{8,12},{10,14},{12,8},{14,10},{16,20},{18,... | collective-permute-start | bytes 3145736 | tf_op jit(solution)/shard_map/ppermute | solution.py:14
  181.0 54.6 %collective-permute-start.7 = (bf16[1024,384]{1,0:T(8,128)(2,1)S(1)}, bf16[1024,384]{1,0:T(8,128)(2,1)S(1)}, u32[]{:S(2)}, u32[]{:S(2)}) collective-permute-start(bf16[1024,384]{1,0:T(8,128)(2,1)S(1)} %get-tuple-element.58), channel_id=1, source_target_pairs={{0,2},{2,0},{4,6},{6,4},{8,10},{10,8},{12,14},{14,12},{16,18},{18,... | collective-permute-start | bytes 2359304 | tf_op jit(solution)/shard_map/ppermute | solution.py:14
  235.7 64.7 %collective-permute-start.37 = (bf16[1024,384]{1,0:T(8,128)(2,1)S(1)}, bf16[1024,384]{1,0:T(8,128)(2,1)S(1)}, u32[]{:S(2)}, u32[]{:S(2)}) collective-permute-start(bf16[1024,384]{1,0:T(8,128)(2,1)S(1)} %get-tuple-element.53), channel_id=1, source_target_pairs={{0,16},{2,18},{4,20},{6,22},{8,24},{10,26},{12,28},{14,30},{16,0},... | collective-permute-start | bytes 2359304 | tf_op jit(solution)/shard_map/ppermute | solution.py:14
  239.8 94.3 %collective-permute-start.41 = (bf16[1024,384]{1,0:T(8,128)(2,1)S(1)}, bf16[1024,384]{1,0:T(8,128)(2,1)S(1)}, u32[]{:S(2)}, u32[]{:S(2)}) collective-permute-start(bf16[1024,384]{1,0:T(8,128)(2,1)S(1)} %get-tuple-element.55), channel_id=1, source_target_pairs={{0,16},{2,18},{4,20},{6,22},{8,24},{10,26},{12,28},{14,30},{16,0},... | collective-permute-start | bytes 2359304 | tf_op jit(solution)/shard_map/ppermute | solution.py:14
  239.9 127.9 %collective-permute-start.45 = (bf16[1024,384]{1,0:T(8,128)(2,1)S(1)}, bf16[1024,384]{1,0:T(8,128)(2,1)S(1)}, u32[]{:S(2)}, u32[]{:S(2)}) collective-permute-start(bf16[1024,384]{1,0:T(8,128)(2,1)S(1)} %get-tuple-element.54), channel_id=1, source_target_pairs={{0,16},{2,18},{4,20},{6,22},{8,24},{10,26},{12,28},{14,30},{16,0},... | collective-permute-start | bytes 2359304 | tf_op jit(solution)/shard_map/ppermute | solution.py:14
  242.9 12.5 %collective-permute-start.26 = (bf16[512,512]{0,1:T(8,128)(2,1)S(1)}, bf16[512,512]{0,1:T(8,128)(2,1)S(1)}, u32[]{:S(2)}, u32[]{:S(2)}) collective-permute-start(bf16[512,512]{0,1:T(8,128)(2,1)S(1)} %slice.200), channel_id=1, source_target_pairs={{0,2},{2,0},{4,6},{6,4},{8,10},{10,8},{12,14},{14,12},{16,18},{18,... | collective-permute-start | bytes 1572872 | tf_op jit(solution)/shard_map/ppermute | solution.py:14
  243.9 12.4 %collective-permute-start.27 = (bf16[512,512]{0,1:T(8,128)(2,1)S(1)}, bf16[512,512]{0,1:T(8,128)(2,1)S(1)}, u32[]{:S(2)}, u32[]{:S(2)}) collective-permute-start(bf16[512,512]{0,1:T(8,128)(2,1)S(1)} %slice.201), channel_id=1, source_target_pairs={{0,4},{2,6},{4,0},{6,2},{8,12},{10,14},{12,8},{14,10},{16,20},{18,... | collective-permute-start | bytes 1572872 | tf_op jit(solution)/shard_map/ppermute | solution.py:14
  255.4 9.2 %collective-permute-start.4 = (bf16[512,512]{1,0:T(8,128)(2,1)S(1)}, bf16[512,512]{1,0:T(8,128)(2,1)S(1)}, u32[]{:S(2)}, u32[]{:S(2)}) collective-permute-start(bf16[512,512]{1,0:T(8,128)(2,1)S(1)} %slice.186), channel_id=1, source_target_pairs={{0,2},{2,0},{4,6},{6,4},{8,10},{10,8},{12,14},{14,12},{16,18},{18,... | collective-permute-start | bytes 1572872 | tf_op jit(solution)/shard_map/ppermute | solution.py:14
  256.2 9.2 %collective-permute-start.5 = (bf16[512,512]{1,0:T(8,128)(2,1)S(1)}, bf16[512,512]{1,0:T(8,128)(2,1)S(1)}, u32[]{:S(2)}, u32[]{:S(2)}) collective-permute-start(bf16[512,512]{1,0:T(8,128)(2,1)S(1)} %slice.187), channel_id=1, source_target_pairs={{0,4},{2,6},{4,0},{6,2},{8,12},{10,14},{12,8},{14,10},{16,20},{18,... | collective-permute-start | bytes 1572872 | tf_op jit(solution)/shard_map/ppermute | solution.py:14
  257.7 2.4 copy-start.7
  264.6 170.7 %collective-permute-start.28 = (bf16[2048,384]{1,0:T(8,128)(2,1)S(1)}, bf16[2048,384]{1,0:T(8,128)(2,1)S(1)}, u32[]{:S(2)}, u32[]{:S(2)}) collective-permute-start(bf16[2048,384]{1,0:T(8,128)(2,1)S(1)} %fusion.3), channel_id=1, source_target_pairs={{0,1},{1,0},{2,3},{3,2},{4,5},{5,4},{6,7},{7,6},{8,9},{9,8},{10,11... | collective-permute-start | bytes 4718600 | tf_op jit(solution)/shard_map/ppermute | solution.py:20
  265.6 2.5 copy-start.3
  267.9 167.4 %collective-permute-start.8 = (bf16[2048,384]{1,0:T(8,128)(2,1)S(1)}, bf16[2048,384]{1,0:T(8,128)(2,1)S(1)}, u32[]{:S(2)}, u32[]{:S(2)}) collective-permute-start(bf16[2048,384]{1,0:T(8,128)(2,1)S(1)} %convolution_convert_fusion.1), channel_id=1, source_target_pairs={{0,1},{1,0},{2,3},{3,2},{4,5},{5,4},{6,7},{7,6},{8,9},{9,8},{10,11... | collective-permute-start | bytes 4718600 | tf_op jit(solution)/shard_map/ppermute | solution.py:20
  300.4 101.1 %collective-permute-start.39 = (bf16[1024,384]{1,0:T(8,128)(2,1)S(1)}, bf16[1024,384]{1,0:T(8,128)(2,1)S(1)}, u32[]{:S(2)}, u32[]{:S(2)}) collective-permute-start(bf16[1024,384]{1,0:T(8,128)(2,1)S(1)} %get-tuple-element.47), channel_id=1, source_target_pairs={{0,16},{2,18},{4,20},{6,22},{8,24},{10,26},{12,28},{14,30},{16,0},... | collective-permute-start | bytes 2359304 | tf_op jit(solution)/shard_map/ppermute | solution.py:14
  334.1 84.3 %collective-permute-start.43 = (bf16[1024,384]{1,0:T(8,128)(2,1)S(1)}, bf16[1024,384]{1,0:T(8,128)(2,1)S(1)}, u32[]{:S(2)}, u32[]{:S(2)}) collective-permute-start(bf16[1024,384]{1,0:T(8,128)(2,1)S(1)} %get-tuple-element.49), channel_id=1, source_target_pairs={{0,16},{2,18},{4,20},{6,22},{8,24},{10,26},{12,28},{14,30},{16,0},... | collective-permute-start | bytes 2359304 | tf_op jit(solution)/shard_map/ppermute | solution.py:14
  367.8 33.7 %copy-start.6 = (bf16[1024,384]{1,0:T(8,128)(2,1)S(1)}, bf16[1024,384]{1,0:T(8,128)(2,1)}, u32[]{:S(2)}) copy-start(bf16[1024,384]{1,0:T(8,128)(2,1)} %get-tuple-element.56) | copy-start | bytes 2359300
  367.8 66.5 %collective-permute-start.47 = (bf16[1024,384]{1,0:T(8,128)(2,1)S(1)}, bf16[1024,384]{1,0:T(8,128)(2,1)S(1)}, u32[]{:S(2)}, u32[]{:S(2)}) collective-permute-start(bf16[1024,384]{1,0:T(8,128)(2,1)S(1)} %get-tuple-element.48), channel_id=1, source_target_pairs={{0,16},{2,18},{4,20},{6,22},{8,24},{10,26},{12,28},{14,30},{16,0},... | collective-permute-start | bytes 2359304 | tf_op jit(solution)/shard_map/ppermute | solution.py:14
  401.5 35.1 %collective-permute-start.10 = (bf16[1024,384]{1,0:T(8,128)(2,1)S(1)}, bf16[1024,384]{1,0:T(8,128)(2,1)S(1)}, u32[]{:S(2)}, u32[]{:S(2)}) collective-permute-start(bf16[1024,384]{1,0:T(8,128)(2,1)S(1)} %copy-done.6), channel_id=1, source_target_pairs={{0,2},{2,0},{4,6},{6,4},{8,10},{10,8},{12,14},{14,12},{16,18},{18,... | collective-permute-start | bytes 2359304 | tf_op jit(solution)/shard_map/ppermute | solution.py:14
  418.4 18.3 %collective-permute-start.42 = (bf16[1024,384]{1,0:T(8,128)(2,1)S(1)}, bf16[1024,384]{1,0:T(8,128)(2,1)S(1)}, u32[]{:S(2)}, u32[]{:S(2)}) collective-permute-start(bf16[1024,384]{1,0:T(8,128)(2,1)S(1)} %get-tuple-element.51), channel_id=1, source_target_pairs={{0,2},{2,0},{4,6},{6,4},{8,10},{10,8},{12,14},{14,12},{16,18},{18,... | collective-permute-start | bytes 2359304 | tf_op jit(solution)/shard_map/ppermute | solution.py:14
  434.6 18.7 %collective-permute-start.44 = (bf16[1024,384]{1,0:T(8,128)(2,1)S(1)}, bf16[1024,384]{1,0:T(8,128)(2,1)S(1)}, u32[]{:S(2)}, u32[]{:S(2)}) collective-permute-start(bf16[1024,384]{1,0:T(8,128)(2,1)S(1)} %get-tuple-element.45), channel_id=1, source_target_pairs={{0,2},{2,0},{4,6},{6,4},{8,10},{10,8},{12,14},{14,12},{16,18},{18,... | collective-permute-start | bytes 2359304 | tf_op jit(solution)/shard_map/ppermute | solution.py:14
  459.7 3.5 collective-permute-start.11
  468.3 14.8 %collective-permute-start.30 = (bf16[512,512]{0,1:T(8,128)(2,1)S(1)}, bf16[512,512]{0,1:T(8,128)(2,1)S(1)}, u32[]{:S(2)}, u32[]{:S(2)}) collective-permute-start(bf16[512,512]{0,1:T(8,128)(2,1)S(1)} %get-tuple-element.29), channel_id=1, source_target_pairs={{0,2},{2,0},{4,6},{6,4},{8,10},{10,8},{12,14},{14,12},{16,18},{18,... | collective-permute-start | bytes 1572872 | tf_op jit(solution)/shard_map/ppermute | solution.py:14
  471.2 70.6 %copy-start.8 = (bf16[2048,1024]{0,1:T(8,128)(2,1)S(1)}, bf16[2048,1024]{0,1:T(8,128)(2,1)}, u32[]{:S(2)}) copy-start(bf16[2048,1024]{0,1:T(8,128)(2,1)} %copy-done.7) | copy-start | bytes 12582916
  471.5 22.9 %collective-permute-start.15 = (bf16[512,512]{0,1:T(8,128)(2,1)S(1)}, bf16[512,512]{0,1:T(8,128)(2,1)S(1)}, u32[]{:S(2)}, u32[]{:S(2)}) collective-permute-start(bf16[512,512]{0,1:T(8,128)(2,1)S(1)} %get-tuple-element.35), channel_id=1, source_target_pairs={{0,2},{2,0},{4,6},{6,4},{8,10},{10,8},{12,14},{14,12},{16,18},{18,... | collective-permute-start | bytes 1572872 | tf_op jit(solution)/shard_map/ppermute | solution.py:14
  473.0 38.2 %collective-permute-start.46 = (bf16[1024,384]{1,0:T(8,128)(2,1)S(1)}, bf16[1024,384]{1,0:T(8,128)(2,1)S(1)}, u32[]{:S(2)}, u32[]{:S(2)}) collective-permute-start(bf16[1024,384]{1,0:T(8,128)(2,1)S(1)} %get-tuple-element.52), channel_id=1, source_target_pairs={{0,2},{2,0},{4,6},{6,4},{8,10},{10,8},{12,14},{14,12},{16,18},{18,... | collective-permute-start | bytes 2359304 | tf_op jit(solution)/shard_map/ppermute | solution.py:14
  473.6 54.5 %collective-permute-start.48 = (bf16[1024,384]{1,0:T(8,128)(2,1)S(1)}, bf16[1024,384]{1,0:T(8,128)(2,1)S(1)}, u32[]{:S(2)}, u32[]{:S(2)}) collective-permute-start(bf16[1024,384]{1,0:T(8,128)(2,1)S(1)} %get-tuple-element.46), channel_id=1, source_target_pairs={{0,2},{2,0},{4,6},{6,4},{8,10},{10,8},{12,14},{14,12},{16,18},{18,... | collective-permute-start | bytes 2359304 | tf_op jit(solution)/shard_map/ppermute | solution.py:14
  475.1 64.2 %collective-permute-start.29 = (bf16[512,512]{0,1:T(8,128)(2,1)S(1)}, bf16[512,512]{0,1:T(8,128)(2,1)S(1)}, u32[]{:S(2)}, u32[]{:S(2)}) collective-permute-start(bf16[512,512]{0,1:T(8,128)(2,1)S(1)} %get-tuple-element.26), channel_id=1, source_target_pairs={{0,2},{2,0},{4,6},{6,4},{8,10},{10,8},{12,14},{14,12},{16,18},{18,... | collective-permute-start | bytes 1572872 | tf_op jit(solution)/shard_map/ppermute | solution.py:14
  483.1 56.7 %collective-permute-start.32 = (bf16[512,512]{0,1:T(8,128)(2,1)S(1)}, bf16[512,512]{0,1:T(8,128)(2,1)S(1)}, u32[]{:S(2)}, u32[]{:S(2)}) collective-permute-start(bf16[512,512]{0,1:T(8,128)(2,1)S(1)} %get-tuple-element.28), channel_id=1, source_target_pairs={{0,4},{2,6},{4,0},{6,2},{8,12},{10,14},{12,8},{14,10},{16,20},{18,... | collective-permute-start | bytes 1572872 | tf_op jit(solution)/shard_map/ppermute | solution.py:14
  494.4 46.5 %collective-permute-start.31 = (bf16[512,512]{0,1:T(8,128)(2,1)S(1)}, bf16[512,512]{0,1:T(8,128)(2,1)S(1)}, u32[]{:S(2)}, u32[]{:S(2)}) collective-permute-start(bf16[512,512]{0,1:T(8,128)(2,1)S(1)} %add_convert_fusion.5), channel_id=1, source_target_pairs={{0,4},{2,6},{4,0},{6,2},{8,12},{10,14},{12,8},{14,10},{16,20},{18,... | collective-permute-start | bytes 1572872 | tf_op jit(solution)/shard_map/ppermute | solution.py:14
  511.2 75.1 %collective-permute-start.38 = (bf16[1024,384]{1,0:T(8,128)(2,1)S(1)}, bf16[1024,384]{1,0:T(8,128)(2,1)S(1)}, u32[]{:S(2)}, u32[]{:S(2)}) collective-permute-start(bf16[1024,384]{1,0:T(8,128)(2,1)S(1)} %get-tuple-element.50), channel_id=1, source_target_pairs={{0,2},{2,0},{4,6},{6,4},{8,10},{10,8},{12,14},{14,12},{16,18},{18,... | collective-permute-start | bytes 2359304 | tf_op jit(solution)/shard_map/ppermute | solution.py:14
  528.1 59.9 %collective-permute-start.40 = (bf16[1024,384]{1,0:T(8,128)(2,1)S(1)}, bf16[1024,384]{1,0:T(8,128)(2,1)S(1)}, u32[]{:S(2)}, u32[]{:S(2)}) collective-permute-start(bf16[1024,384]{1,0:T(8,128)(2,1)S(1)} %get-tuple-element.44), channel_id=1, source_target_pairs={{0,2},{2,0},{4,6},{6,4},{8,10},{10,8},{12,14},{14,12},{16,18},{18,... | collective-permute-start | bytes 2359304 | tf_op jit(solution)/shard_map/ppermute | solution.py:14
  539.3 44.1 %collective-permute-start.14 = (bf16[512,512]{0,1:T(8,128)(2,1)S(1)}, bf16[512,512]{0,1:T(8,128)(2,1)S(1)}, u32[]{:S(2)}, u32[]{:S(2)}) collective-permute-start(bf16[512,512]{0,1:T(8,128)(2,1)S(1)} %get-tuple-element.32), channel_id=1, source_target_pairs={{0,2},{2,0},{4,6},{6,4},{8,10},{10,8},{12,14},{14,12},{16,18},{18,... | collective-permute-start | bytes 1572872 | tf_op jit(solution)/shard_map/ppermute | solution.py:14
  539.8 43.7 %collective-permute-start.17 = (bf16[512,512]{0,1:T(8,128)(2,1)S(1)}, bf16[512,512]{0,1:T(8,128)(2,1)S(1)}, u32[]{:S(2)}, u32[]{:S(2)}) collective-permute-start(bf16[512,512]{0,1:T(8,128)(2,1)S(1)} %get-tuple-element.34), channel_id=1, source_target_pairs={{0,4},{2,6},{4,0},{6,2},{8,12},{10,14},{12,8},{14,10},{16,20},{18,... | collective-permute-start | bytes 1572872 | tf_op jit(solution)/shard_map/ppermute | solution.py:14
  540.8 44.6 %collective-permute-start.16 = (bf16[512,512]{0,1:T(8,128)(2,1)S(1)}, bf16[512,512]{0,1:T(8,128)(2,1)S(1)}, u32[]{:S(2)}, u32[]{:S(2)}) collective-permute-start(bf16[512,512]{0,1:T(8,128)(2,1)S(1)} %add_convert_fusion.10), channel_id=1, source_target_pairs={{0,4},{2,6},{4,0},{6,2},{8,12},{10,14},{12,8},{14,10},{16,20},{18,... | collective-permute-start | bytes 1572872 | tf_op jit(solution)/shard_map/ppermute | solution.py:14
  583.5 14.9 %collective-permute-start.34 = (bf16[512,512]{0,1:T(8,128)(2,1)S(1)}, bf16[512,512]{0,1:T(8,128)(2,1)S(1)}, u32[]{:S(2)}, u32[]{:S(2)}) collective-permute-start(bf16[512,512]{0,1:T(8,128)(2,1)S(1)} %get-tuple-element.27), channel_id=1, source_target_pairs={{0,4},{2,6},{4,0},{6,2},{8,12},{10,14},{12,8},{14,10},{16,20},{18,... | collective-permute-start | bytes 1572872 | tf_op jit(solution)/shard_map/ppermute | solution.py:14
  583.5 24.3 %collective-permute-start.19 = (bf16[512,512]{0,1:T(8,128)(2,1)S(1)}, bf16[512,512]{0,1:T(8,128)(2,1)S(1)}, u32[]{:S(2)}, u32[]{:S(2)}) collective-permute-start(bf16[512,512]{0,1:T(8,128)(2,1)S(1)} %get-tuple-element.33), channel_id=1, source_target_pairs={{0,4},{2,6},{4,0},{6,2},{8,12},{10,14},{12,8},{14,10},{16,20},{18,... | collective-permute-start | bytes 1572872 | tf_op jit(solution)/shard_map/ppermute | solution.py:14
  585.5 14.9 %collective-permute-start.33 = (bf16[512,512]{0,1:T(8,128)(2,1)S(1)}, bf16[512,512]{0,1:T(8,128)(2,1)S(1)}, u32[]{:S(2)}, u32[]{:S(2)}) collective-permute-start(bf16[512,512]{0,1:T(8,128)(2,1)S(1)} %get-tuple-element.25), channel_id=1, source_target_pairs={{0,2},{2,0},{4,6},{6,4},{8,10},{10,8},{12,14},{14,12},{16,18},{18,... | collective-permute-start | bytes 1572872 | tf_op jit(solution)/shard_map/ppermute | solution.py:14
  586.4 22.9 %collective-permute-start.18 = (bf16[512,512]{0,1:T(8,128)(2,1)S(1)}, bf16[512,512]{0,1:T(8,128)(2,1)S(1)}, u32[]{:S(2)}, u32[]{:S(2)}) collective-permute-start(bf16[512,512]{0,1:T(8,128)(2,1)S(1)} %get-tuple-element.31), channel_id=1, source_target_pairs={{0,2},{2,0},{4,6},{6,4},{8,10},{10,8},{12,14},{14,12},{16,18},{18,... | collective-permute-start | bytes 1572872 | tf_op jit(solution)/shard_map/ppermute | solution.py:14
  600.6 13.8 %collective-permute-start.35 = (bf16[256,1024]{0,1:T(8,128)(2,1)S(1)}, bf16[256,1024]{0,1:T(8,128)(2,1)S(1)}, u32[]{:S(2)}, u32[]{:S(2)}) collective-permute-start(bf16[256,1024]{0,1:T(8,128)(2,1)S(1)} %pad_maximum_fusion.1), channel_id=1, source_target_pairs={{0,8},{2,10},{4,12},{6,14},{8,0},{10,2},{12,4},{14,6},{16,24},{18,... | collective-permute-start | bytes 1572872 | tf_op jit(solution)/shard_map/ppermute | solution.py:14
  609.6 17.4 %collective-permute-start.20 = (bf16[256,1024]{0,1:T(8,128)(2,1)S(1)}, bf16[256,1024]{0,1:T(8,128)(2,1)S(1)}, u32[]{:S(2)}, u32[]{:S(2)}) collective-permute-start(bf16[256,1024]{0,1:T(8,128)(2,1)S(1)} %pad_maximum_fusion.2), channel_id=1, source_target_pairs={{0,8},{2,10},{4,12},{6,14},{8,0},{10,2},{12,4},{14,6},{16,24},{18,... | collective-permute-start | bytes 1572872 | tf_op jit(solution)/shard_map/ppermute | solution.py:14
  614.6 16.5 %collective-permute-start.36 = (bf16[128,1024]{0,1:T(8,128)(2,1)S(1)}, bf16[128,1024]{0,1:T(8,128)(2,1)S(1)}, u32[]{:S(2)}, u32[]{:S(2)}) collective-permute-start(bf16[128,1024]{0,1:T(8,128)(2,1)S(1)} %slice.213), channel_id=1, source_target_pairs={{0,16},{2,18},{4,20},{6,22},{8,24},{10,26},{12,28},{14,30},{16,0},... | collective-permute-start | bytes 786440 | tf_op jit(solution)/shard_map/ppermute | solution.py:14
  627.1 13.5 %collective-permute-start.21 = (bf16[128,1024]{0,1:T(8,128)(2,1)S(1)}, bf16[128,1024]{0,1:T(8,128)(2,1)S(1)}, u32[]{:S(2)}, u32[]{:S(2)}) collective-permute-start(bf16[128,1024]{0,1:T(8,128)(2,1)S(1)} %slice.199), channel_id=1, source_target_pairs={{0,16},{2,18},{4,20},{6,22},{8,24},{10,26},{12,28},{14,30},{16,0},... | collective-permute-start | bytes 786440 | tf_op jit(solution)/shard_map/ppermute | solution.py:14
